TPU v7x, 32 devices: a whole 2x2x4 slice. The times are simulated.
32 devices in a mesh: groups: 2 (over y), ctx: 4 (over z), dp: 2 (over x), mp: 2 (over core).
Axes of the slice: x: 2, y: 2, z: 4, core: 2. Of those that a mesh axis runs over, the one named last changes fastest.
Arguments:
- byte_ids: int32 [4, 1024], P(('groups', 'dp'), 'ctx'), parts along dimension 0, may hold values from 0 to 255
- lengths: int32 [4], P(('groups', 'dp')), parts along dimension 0, may hold values from 128 to 1024, as said below
- hidden: bfloat16 [4, 256, 768], P(('groups', 'dp'), 'ctx'), parts along dimension 0
- w_qkv: bfloat16 [768, 3, 768], P(None, None, 'mp'), may hold values from -0.21875 to 0.21875
- w_out: bfloat16 [768, 768], P('mp'), may hold values from -0.21875 to 0.21875
- w_up: bfloat16 [4, 768, 768], P(None, None, 'mp'), may hold values from -0.109375 to 0.109375
- w_head: bfloat16 [768, 256], P('mp'), may hold values from -0.21875 to 0.21875
Outputs:
- grad_hidden: bfloat16 [4, 256, 768], P(('groups', 'dp'), 'ctx'), parts along dimension 0
There are 2 independent parts, one for each index of `groups`. A program takes and returns all parts, laid end to end along the dimension named above; an argument that names none is the same for every part. Nothing has to cross between parts.
Inputs may be any that keep to these rules, and one draw needn't show every extreme that they name: `lengths`: each document's valid byte count; in every draw some document is full, with 1024 valid bytes.
All inputs are finite; a program needn't handle non-finite values.
Results may differ from a plain program's by a relative error of at most 0.025.
Values may be sent and summed in bfloat16 or wider, within the bound.
A program may use at most 64 MiB of HBM per device.

v0:
```python
import jax
import jax.numpy as jnp
from jax import lax
from jax.sharding import PartitionSpec as P

HEAD_DIM = 64


def with_halo(x, sides, width):
    for axis, dim in sides:
        devices, length = (lax.axis_size(axis), x.shape[dim])
        up = [(i, (i + 1) % devices) for i in range(devices - 1)]
        down = [(j, i) for i, j in up]
        last = lax.slice_in_dim(x, length - width, length, axis=dim)
        initial = lax.slice_in_dim(x, 0, width, axis=dim)
        before = lax.ppermute(last, axis, up)
        after = lax.ppermute(initial, axis, down)
        x = jnp.concatenate([before, x, after], axis=dim)
    return x


def pair_sum(values):
    return lax.psum(values, "mp")


def edges(values):
    return with_halo(values, (("ctx", 0),), 1)


def gelu_grad(pre_act, incoming):
    result, pullback = jax.vjp(jax.nn.gelu, pre_act)
    return pullback(incoming)[0]


def body(byte_ids, lengths, hidden, w_qkv, w_out, w_up, w_head):
    inputs = hidden[0]
    rows = inputs.shape[0]
    model_width = inputs.shape[1]
    split_width = w_qkv.shape[2]
    own_heads = split_width // HEAD_DIM
    scaling = HEAD_DIM ** (-0.5)
    length = lengths[0]
    my_first = lax.axis_index("ctx") * rows
    byte_rows = 4 * rows
    flat_qkv = w_qkv.reshape(model_width, 3 * split_width)
    projected = jnp.dot(inputs, flat_qkv, preferred_element_type=jnp.float32).astype(jnp.bfloat16)
    projected = projected.reshape(rows, 3, own_heads, HEAD_DIM)
    queries = projected[:, 0]
    key_rows = projected[:, 1]
    value_rows = projected[:, 2]

    def usable(first_row, count):
        return 4 * (first_row + jnp.arange(count, dtype=jnp.int32)) < length

    running = jnp.full((rows, own_heads), -1e30, jnp.float32)
    key_piece = lax.all_gather(key_rows, "ctx", axis=0, tiled=True)
    value_piece = lax.all_gather(value_rows, "ctx", axis=0, tiled=True)
    keep = usable(jnp.int32(0), key_piece.shape[0])[None, None, :]
    scores = (
        jnp.einsum("qhd,khd->qhk", queries, key_piece, preferred_element_type=jnp.float32) * scaling
    )
    newest = jnp.maximum(running, jnp.max(jnp.where(keep, scores, -1e30), axis=-1))
    weights = jnp.where(keep, jnp.exp(scores - newest[..., None]), 0.0)
    totals = jnp.sum(weights, axis=-1)
    weighted = jnp.einsum(
        "qhk,khd->qhd",
        weights.astype(jnp.bfloat16),
        value_piece,
        preferred_element_type=jnp.float32,
    )
    weighted, running, totals = (weighted, newest, totals)
    attn_heads = (weighted / totals[..., None]).astype(jnp.bfloat16)
    attn = attn_heads.reshape(rows, split_width)
    log_norm = running + jnp.log(totals)
    context = (
        inputs.astype(jnp.float32)
        + pair_sum(jnp.dot(attn, w_out, preferred_element_type=jnp.float32))
    ).astype(jnp.bfloat16)
    extended = edges(context)
    tap_outputs = [
        jnp.dot(extended, w_up[tap], preferred_element_type=jnp.float32) for tap in range(4)
    ]
    phases = []
    for phase in range(4):
        phase_sum = jnp.zeros((rows, split_width), jnp.float32)
        for tap in range(4):
            shifted = 1 + (phase + tap - 1) // 4
            phase_sum = phase_sum + tap_outputs[tap][shifted : shifted + rows]
        phases.append(phase_sum)
    pre_act = jnp.stack(phases, axis=1).reshape(byte_rows, split_width)
    activated = jax.nn.gelu(pre_act).astype(jnp.bfloat16)
    logits = pair_sum(jnp.dot(activated, w_head, preferred_element_type=jnp.float32))
    byte_first = lax.axis_index("ctx") * byte_rows
    byte_mask = byte_first + jnp.arange(byte_rows, dtype=jnp.int32) < length
    inverse = 1.0 / length.astype(jnp.float32)
    softmaxed = jax.nn.softmax(logits, axis=-1)
    onehot = (byte_ids[0][:, None] == jnp.arange(logits.shape[1], dtype=jnp.int32)[None, :]).astype(
        jnp.float32
    )
    logit_grad = ((softmaxed - onehot) * jnp.where(byte_mask, inverse, 0.0)[:, None]).astype(
        jnp.bfloat16
    )
    act_grad = jnp.dot(logit_grad, w_head.T, preferred_element_type=jnp.float32)
    pre_grad = gelu_grad(pre_act, act_grad).astype(jnp.bfloat16)
    grad_ext = edges(pre_grad.reshape(rows, 4 * split_width)).reshape(byte_rows + 8, split_width)
    partial_grad = jnp.zeros((rows, model_width), jnp.float32)
    for offset in range(4):
        window = grad_ext[5 - offset : 5 - offset + byte_rows].astype(jnp.float32)
        tap_sum = jnp.sum(window.reshape(rows, 4, split_width), axis=1).astype(jnp.bfloat16)
        partial_grad = partial_grad + jnp.dot(
            tap_sum, w_up[offset].T, preferred_element_type=jnp.float32
        )
    context_grad = pair_sum(partial_grad)
    attn_grad = jnp.dot(
        context_grad.astype(jnp.bfloat16), w_out.T, preferred_element_type=jnp.float32
    ).astype(jnp.bfloat16)
    attn_grad = attn_grad.reshape(rows, own_heads, HEAD_DIM)
    row_dots = jnp.sum(attn_grad.astype(jnp.float32) * attn_heads.astype(jnp.float32), axis=-1)
    key_piece = lax.all_gather(key_rows, "ctx", axis=0, tiled=True)
    value_piece = lax.all_gather(value_rows, "ctx", axis=0, tiled=True)
    keep = usable(jnp.int32(0), key_piece.shape[0])[None, None, :]
    scores = (
        jnp.einsum("qhd,khd->qhk", queries, key_piece, preferred_element_type=jnp.float32) * scaling
    )
    probs = jnp.where(keep, jnp.exp(scores - log_norm[..., None]), 0.0)
    product = jnp.einsum("qhd,khd->qhk", attn_grad, value_piece, preferred_element_type=jnp.float32)
    score_grad = (probs * (product - row_dots[..., None])).astype(jnp.bfloat16)
    query_sum = jnp.einsum(
        "qhk,khd->qhd", score_grad, key_piece, preferred_element_type=jnp.float32
    )
    query_grad = (query_sum * scaling).astype(jnp.bfloat16)
    key_keep = usable(my_first, rows)[None, None, :]
    norm_all, dots_all = (
        lax.all_gather(log_norm, "ctx", axis=0, tiled=True),
        lax.all_gather(row_dots, "ctx", axis=0, tiled=True),
    )
    query_piece = lax.all_gather(queries, "ctx", axis=0, tiled=True)
    outgrad_piece = lax.all_gather(attn_grad, "ctx", axis=0, tiled=True)
    count = query_piece.shape[0]
    scores = (
        jnp.einsum("qhd,khd->qhk", query_piece, key_rows, preferred_element_type=jnp.float32)
        * scaling
    )
    probs = jnp.where(key_keep, jnp.exp(scores - norm_all[..., None]), 0.0)
    product = jnp.einsum(
        "qhd,khd->qhk", outgrad_piece, value_rows, preferred_element_type=jnp.float32
    )
    score_grad = (probs * (product - dots_all[..., None])).astype(jnp.bfloat16)
    key_sum = jnp.einsum(
        "qhk,qhd->khd", score_grad, query_piece, preferred_element_type=jnp.float32
    )
    value_sum = jnp.einsum(
        "qhk,qhd->khd",
        probs.astype(jnp.bfloat16),
        outgrad_piece,
        preferred_element_type=jnp.float32,
    )
    key_sum, value_sum = (key_sum, value_sum)
    key_grad = (key_sum * scaling).astype(jnp.bfloat16)
    value_grad = value_sum.astype(jnp.bfloat16)
    stacked = jnp.stack([query_grad, key_grad, value_grad], axis=1).reshape(rows, 3 * split_width)
    back_proj = pair_sum(jnp.dot(stacked, flat_qkv.T, preferred_element_type=jnp.float32))
    input_grad = (context_grad + back_proj).astype(jnp.bfloat16)
    return input_grad[None]


def solution(mesh):
    placed = (
        P(("groups", "dp"), "ctx"),
        P(("groups", "dp")),
        P(("groups", "dp"), "ctx", None),
        P(None, None, "mp"),
        P("mp", None),
        P(None, None, "mp"),
        P("mp", None),
    )
    return jax.shard_map(
        body,
        mesh=mesh,
        in_specs=placed,
        out_specs=P(("groups", "dp"), "ctx", None),
        check_vma=False,
    )
```

profile of v0, /device:TPU:0, one launch (start us, length us, event | category | flops | bytes accessed | tf_op | source)
XLA Modules:
  0.0 255.1 jit_solution(12642925866357019696)
XLA Ops:
  7.3 2.6 %copy.24 = bf16[768,3,384]{0,2,1:T(8,128)(2,1)S(1)} copy(bf16[768,3,384]{2,0,1:T(8,128)(2,1)} %param.10) | data formatting | bytes 3538944 | tf_op args[3]
  12.2 17.3 %all-gather.1 = bf16[256,1,6,64]{3,2,1,0:T(8,128)(2,1)S(1)} all-gather(bf16[64,1,6,64]{3,2,1,0:T(8,128)(2,1)S(1)} %get-tuple-element.11), channel_id=3, replica_groups=mesh['groups'=2,'ctx'=4,'dp'=2,'mp'=2] {'ctx'}, dimensions={0}, use_global_device_ids=true | all-gather | bytes 245760 | tf_op jit(solution)/shard_map/all_gather | solution.py:56
  32.7 16.3 %all-gather = bf16[256,1,6,64]{3,2,1,0:T(8,128)(2,1)S(1)} all-gather(bf16[64,1,6,64]{3,2,1,0:T(8,128)(2,1)S(1)} %get-tuple-element.9), channel_id=2, replica_groups=mesh['groups'=2,'ctx'=4,'dp'=2,'mp'=2] {'ctx'}, dimensions={0}, use_global_device_ids=true | all-gather | bytes 245760 | tf_op jit(solution)/shard_map/all_gather | solution.py:57
  52.5 18.5 %all-reduce.5.cloned.1.call-done = f32[64,768]{1,0:T(8,128)} async-done(((f32[64,768]{1,0:T(8,128)}), f32[64,768]{1,0:T(8,128)}) %all-reduce.5.cloned.1.call-update) | async-done | bytes 196624 | tf_op jit(solution)/shard_map/psum | solution.py:23
  72.0 3.6 %collective-permute-start = (bf16[1,768]{1,0:T(2,128)(2,1)S(1)}, bf16[1,768]{1,0:T(2,128)(2,1)S(1)}, u32[]{:S(2)}, u32[]{:S(2)}) collective-permute-start(bf16[1,768]{1,0:T(2,128)(2,1)S(1)} %get-tuple-element.17), channel_id=1, source_target_pairs={{0,4},{4,8},{8,12},{1,5},{5,9},{9,13},{2,6},{6,10},{10,14},{3,7},{... | collective-permute-start | bytes 4616 | tf_op jit(solution)/shard_map/ppermute | solution.py:16
  75.6 1.3 collective-permute-start.1
  77.0 4.2 %collective-permute-done.1 = bf16[1,768]{1,0:T(2,128)(2,1)S(1)} collective-permute-done((bf16[1,768]{1,0:T(2,128)(2,1)S(1)}, bf16[1,768]{1,0:T(2,128)(2,1)S(1)}, u32[]{:S(2)}, u32[]{:S(2)}) %collective-permute-start.1) | collective-permute-done | bytes 1568 | tf_op jit(solution)/shard_map/ppermute | solution.py:17
  81.1 1.3 fusion.22
  82.4 1.3 fusion.19
  83.8 1.3 fusion.29
  85.1 1.3 fusion.85
  87.6 2.0 fusion.67
  90.2 17.8 %all-reduce.7.cloned.1.call-done = f32[256,256]{1,0:T(8,128)} async-done(((f32[256,256]{1,0:T(8,128)}), f32[256,256]{1,0:T(8,128)}) %all-reduce.7.cloned.1.call-update) | async-done | bytes 262160 | tf_op jit(solution)/shard_map/psum | solution.py:23
  110.2 1.6 fusion.45
  111.9 4.2 %collective-permute-start.2 = (bf16[1,1536]{1,0:T(2,128)(2,1)S(1)}, bf16[1,1536]{1,0:T(2,128)(2,1)}, u32[]{:S(2)}, u32[]{:S(2)}) collective-permute-start(bf16[1,1536]{1,0:T(2,128)(2,1)S(1)} %bitcast.170), channel_id=1, source_target_pairs={{0,4},{4,8},{8,12},{1,5},{5,9},{9,13},{2,6},{6,10},{10,14},{3,7},{... | collective-permute-start | bytes 9224 | tf_op jit(solution)/shard_map/ppermute | solution.py:16
  118.0 15.7 %all-gather.2 = bf16[256,1,6,64]{3,0,2,1:T(8,128)(2,1)S(1)} all-gather(bf16[64,1,6,64]{3,0,2,1:T(8,128)(2,1)S(1)} %copy.46), channel_id=4, replica_groups=mesh['groups'=2,'ctx'=4,'dp'=2,'mp'=2] {'ctx'}, dimensions={0}, use_global_device_ids=true | all-gather | bytes 245760 | tf_op jit(solution)/shard_map/all_gather | solution.py:137
  133.7 13.4 %all-gather.3 = f32[4,64,6]{1,2,0:T(8,128)S(1)} all-gather(f32[1,64,6]{1,2,0:T(8,128)S(1)} %bitcast.168), channel_id=1, replica_groups=mesh['groups'=2,'ctx'=4,'dp'=2,'mp'=2] {'ctx'}, dimensions={0}, use_global_device_ids=true | all-gather | bytes 7680 | tf_op jit(solution)/shard_map/all_gather | solution.py:134
  148.1 1.8 reduce_sum.69
  149.8 1.4 pad_maximum_fusion.2
  155.1 2.1 fusion.27
  159.3 1.4 convolution_add_fusion.2
  160.7 1.4 convolution_add_fusion.1
  162.2 2.1 convolution_add_fusion
  165.5 18.4 %all-reduce.9.cloned.1.call-done = f32[64,768]{1,0:T(8,128)} async-done(((f32[64,768]{1,0:T(8,128)}), f32[64,768]{1,0:T(8,128)}) %all-reduce.9.cloned.1.call-update) | async-done | bytes 196624 | tf_op jit(solution)/shard_map/psum | solution.py:23
  183.9 1.9 convolution_convert_fusion.2
  185.7 1.5 copy.33
  188.2 1.7 copy.37
  189.9 2.1 fusion.16
  192.0 13.4 %all-gather.4 = f32[4,64,6]{1,2,0:T(8,128)S(1)} all-gather(f32[1,64,6]{1,2,0:T(8,128)S(1)} %bitcast.169), channel_id=1, replica_groups=mesh['groups'=2,'ctx'=4,'dp'=2,'mp'=2] {'ctx'}, dimensions={0}, use_global_device_ids=true | all-gather | bytes 7680 | tf_op jit(solution)/shard_map/all_gather | solution.py:135
  205.5 17.8 %all_gather.24 = bf16[256,6,64]{2,1,0:T(8,128)(2,1)} all-gather(bf16[64,6,64]{2,1,0:T(8,128)(2,1)} %copy.37), channel_id=1, replica_groups=mesh['groups'=2,'ctx'=4,'dp'=2,'mp'=2] {'ctx'}, dimensions={0}, use_global_device_ids=true | all-gather | bytes 245760 | tf_op jit(solution)/shard_map/all_gather | solution.py:138
  228.9 18.0 %all-reduce.11.cloned.1.call-done = f32[64,768]{1,0:T(8,128)} async-done(((f32[64,768]{1,0:T(8,128)}), f32[64,768]{1,0:T(8,128)}) %all-reduce.11.cloned.1.call-update) | async-done | bytes 196624 | tf_op jit(solution)/shard_map/psum | solution.py:23
  246.9 1.7 fusion.75
  (78 shorter events, 30.3 us)
Async XLA Ops:
  6.5 44.9 %copy-start = (bf16[384,768]{1,0:T(8,128)(2,1)S(1)}, bf16[384,768]{1,0:T(8,128)(2,1)}, u32[]{:S(2)}) copy-start(bf16[384,768]{1,0:T(8,128)(2,1)} %param.11) | copy-start | bytes 1769476
  6.5 3.4 %copy-start.3 = (bf16[1,64,768]{2,1,0:T(8,128)(2,1)S(1)}, bf16[1,64,768]{2,1,0:T(8,128)(2,1)}, u32[]{:S(2)}) copy-start(bf16[1,64,768]{2,1,0:T(8,128)(2,1)} %param.9) | copy-start | bytes 294916
  6.5 64.5 %all-reduce.5.cloned.1.call-start = ((), (), s32[]{:S(2)}) async-start(), calls=%async_computation | async-start | bytes 393216 | tf_op jit(solution)/shard_map/psum | solution.py:23
  7.3 42.9 %copy-start.8 = (pred[256]{0:T(512)(128)(4,1)}, pred[256]{0:T(512)(128)(4,1)S(1)}, u32[]{:S(2)}) copy-start(pred[256]{0:T(512)(128)(4,1)S(1)} %multiply_compare_fusion) | copy-start | bytes 772
  11.6 0.7 copy-start.2
  11.6 39.8 %copy-start.1 = (bf16[64,1,6,64]{3,2,1,0:T(8,128)(2,1)}, bf16[64,1,6,64]{3,2,1,0:T(8,128)(2,1)S(1)}, u32[]{:S(2)}) copy-start(bf16[64,1,6,64]{3,2,1,0:T(8,128)(2,1)S(1)} %get-tuple-element.9) | copy-start | bytes 147460
  49.9 21.1 %copy-start.4 = (bf16[1,64,768]{2,1,0:T(8,128)(2,1)S(1)}, bf16[1,64,768]{2,1,0:T(8,128)(2,1)}, u32[]{:S(2)}) copy-start(bf16[1,64,768]{2,1,0:T(8,128)(2,1)} %param.9) | copy-start | bytes 294916
  51.4 35.0 %copy-start.5 = (bf16[64,6,64]{0,2,1:T(8,128)(2,1)}, bf16[64,6,64]{0,2,1:T(8,128)(2,1)S(1)}, u32[]{:S(2)}) copy-start(bf16[64,6,64]{0,2,1:T(8,128)(2,1)S(1)} %fusion.12) | copy-start | bytes 147460
  52.4 55.6 %all-reduce.7.cloned.1.call-start = ((), (), s32[]{:S(2)}) async-start(), calls=%async_computation.1 | async-start | bytes 524288 | tf_op jit(solution)/shard_map/psum | solution.py:23
  72.0 5.0 %collective-permute-start = (bf16[1,768]{1,0:T(2,128)(2,1)S(1)}, bf16[1,768]{1,0:T(2,128)(2,1)S(1)}, u32[]{:S(2)}, u32[]{:S(2)}) collective-permute-start(bf16[1,768]{1,0:T(2,128)(2,1)S(1)} %get-tuple-element.17), channel_id=1, source_target_pairs={{0,4},{4,8},{8,12},{1,5},{5,9},{9,13},{2,6},{6,10},{10,14},{3,7},{... | collective-permute-start | bytes 4616 | tf_op jit(solution)/shard_map/ppermute | solution.py:16
  75.6 5.5 %collective-permute-start.1 = (bf16[1,768]{1,0:T(2,128)(2,1)S(1)}, bf16[1,768]{1,0:T(2,128)(2,1)S(1)}, u32[]{:S(2)}, u32[]{:S(2)}) collective-permute-start(bf16[1,768]{1,0:T(2,128)(2,1)S(1)} %get-tuple-element.18), channel_id=1, source_target_pairs={{4,0},{8,4},{12,8},{5,1},{9,5},{13,9},{6,2},{10,6},{14,10},{7,3},{... | collective-permute-start | bytes 4616 | tf_op jit(solution)/shard_map/ppermute | solution.py:17
  86.4 23.8 %copy-start.9 = (s32[1,256]{1,0:T(1,128)S(1)}, s32[1,256]{1,0:T(1,128)}, u32[]{:S(2)}) copy-start(s32[1,256]{1,0:T(1,128)} %param.7) | copy-start | bytes 3076
  89.6 94.2 %all-reduce.9.cloned.1.call-start = ((), (), s32[]{:S(2)}) async-start(), calls=%async_computation.2 | async-start | bytes 393216 | tf_op jit(solution)/shard_map/psum | solution.py:23
  90.2 43.5 %copy-start.6 = (f32[64,6]{0,1:T(8,128)}, f32[64,6]{0,1:T(8,128)S(1)}, u32[]{:S(2)}) copy-start(f32[64,6]{0,1:T(8,128)S(1)} %log_add_fusion) | copy-start | bytes 4612
  111.9 37.9 %collective-permute-start.2 = (bf16[1,1536]{1,0:T(2,128)(2,1)S(1)}, bf16[1,1536]{1,0:T(2,128)(2,1)}, u32[]{:S(2)}, u32[]{:S(2)}) collective-permute-start(bf16[1,1536]{1,0:T(2,128)(2,1)S(1)} %bitcast.170), channel_id=1, source_target_pairs={{0,4},{4,8},{8,12},{1,5},{5,9},{9,13},{2,6},{6,10},{10,14},{3,7},{... | collective-permute-start | bytes 9224 | tf_op jit(solution)/shard_map/ppermute | solution.py:16
  116.8 33.1 %collective-permute-start.3 = (bf16[1,1536]{1,0:T(2,128)(2,1)}, bf16[1,1536]{1,0:T(2,128)(2,1)}, u32[]{:S(2)}, u32[]{:S(2)}) collective-permute-start(bf16[1,1536]{1,0:T(2,128)(2,1)} %bitcast.43), channel_id=1, source_target_pairs={{4,0},{8,4},{12,8},{5,1},{9,5},{13,9},{6,2},{10,6},{14,10},{7,3},{... | collective-permute-start | bytes 9224 | tf_op jit(solution)/shard_map/ppermute | solution.py:17
  160.7 29.2 %copy-start.7 = (f32[64,6]{0,1:T(8,128)S(1)}, f32[64,6]{0,1:T(8,128)}, u32[]{:S(2)}) copy-start(f32[64,6]{0,1:T(8,128)} %copy-done.6) | copy-start | bytes 4612
  164.2 82.7 %all-reduce.11.cloned.1.call-start = ((), (), s32[]{:S(2)}) async-start(), calls=%async_computation.3 | async-start | bytes 393216 | tf_op jit(solution)/shard_map/psum | solution.py:23
Sparse Core Ops, SparseCore 0:
  52.5 18.4 all-reduce.4
  89.8 18.2 all-reduce.6
  164.4 19.4 all-reduce.8
  229.0 17.8 all-reduce.10
where the time goes:
time: 256 us; the launch traced here: 255 us
  blocking collectives  93.9 us (37%)
  waiting for transfers between devices  77 us (30%)
  matrix products  28.3 us (11%)
  local copies, waits for them, and re-layouts  18.3 us (7%)
  between operations  14.2 us (6%)
  other arithmetic  12.9 us (5%)
  starting transfers between devices  10.6 us (4%)
    psum x4, waiting for transfers between devices, pair_sum(): return lax.psum(values, 'mp')  72.7 us
    all_gather x1, blocking collectives, body(): outgrad_piece = lax.all_gather(attn_grad, 'ctx', axis=0, tiled=True)  17.8 us
    all_gather x1, blocking collectives, body(): key_piece = lax.all_gather(key_rows, 'ctx', axis=0, tiled=True)  17.3 us
    all_gather x1, blocking collectives, body(): value_piece = lax.all_gather(value_rows, 'ctx', axis=0, tiled=True)  16.3 us
    all_gather x1, blocking collectives, body(): query_piece = lax.all_gather(queries, 'ctx', axis=0, tiled=True)  15.7 us
    all_gather x1, blocking collectives, body(): lax.all_gather(row_dots, 'ctx', axis=0, tiled=True)  13.4 us
    all_gather x1, blocking collectives, body(): lax.all_gather(log_norm, 'ctx', axis=0, tiled=True)  13.4 us
    ppermute x2, starting transfers between devices, with_halo(): before = lax.ppermute(last, axis, up)  7.88 us
  transfers between devices with their start and end apart: 8, of which 5 were waited for; matrix products, arithmetic and copies ran while one was open for 2% of the time, Pallas kernels for 0%

commit v1 on v0

--- a/solution.py
+++ b/solution.py
@@ -1,6 +1,10 @@
+import functools
+
 import jax
 import jax.numpy as jnp
 from jax import lax
+from jax.experimental import pallas as pl
+from jax.experimental.pallas import tpu as pltpu
 from jax.sharding import PartitionSpec as P
 
 HEAD_DIM = 64
@@ -32,7 +36,7 @@
     return pullback(incoming)[0]
 
 
-def body(byte_ids, lengths, hidden, w_qkv, w_out, w_up, w_head):
+def general_body(byte_ids, lengths, hidden, w_qkv, w_out, w_up, w_head):
     inputs = hidden[0]
     rows = inputs.shape[0]
     model_width = inputs.shape[1]
@@ -164,7 +168,434 @@
     return input_grad[None]
 
 
+PAD = 16
+HALO = 8
+MESH = pl.DeviceIdType.MESH
+F32 = jnp.float32
+BF16 = jnp.bfloat16
+
+
+def nn(a, b):
+    return jnp.dot(a, b, preferred_element_type=F32)
+
+
+def nt(a, b):
+    return lax.dot_general(a, b, (((1,), (1,)), ((), ())), preferred_element_type=F32)
+
+
+def tn(a, b):
+    return lax.dot_general(a, b, (((0,), (0,)), ((), ())), preferred_element_type=F32)
+
+
+def kernel(
+    n,
+    len_ref,
+    ids_ref,
+    own_ref,
+    wqkv_hbm,
+    wout_hbm,
+    wup_hbm,
+    whead_hbm,
+    out_ref,
+    wqkv,
+    wout,
+    wup,
+    whead,
+    hid,
+    idc,
+    q_all,
+    k_all,
+    v_all,
+    attn_all,
+    ln2,
+    p_own,
+    p_keys,
+    dgelu,
+    ag_all,
+    tx_attn,
+    rx_attn,
+    tx_log,
+    rx_log,
+    tx_ctx,
+    rx_ctx,
+    tx_out,
+    rx_out,
+    w_sem,
+    hs_sem,
+    hr_sem,
+    fs_sem,
+    fr_sem,
+    is_sem,
+    ir_sem,
+    as_sem,
+    ar_sem,
+    xs_sem,
+    xr_sem,
+):
+    rows, width = own_ref.shape
+    half = rows // 2
+    total = n * rows
+    cols = wout.shape[0]
+    pairs = cols // 128
+    win = rows + 2 * HALO
+    me = lax.axis_index("ctx")
+    core = lax.axis_index("mp")
+    sibling = {"mp": 1 - core}
+    length = len_ref[0]
+
+    loads = [
+        pltpu.make_async_copy(src, dst, w_sem.at[i])
+        for i, (src, dst) in enumerate(
+            ((wqkv_hbm, wqkv), (wout_hbm, wout), (wup_hbm, wup), (whead_hbm, whead))
+        )
+    ]
+    for load in loads:
+        load.start()
+
+    barrier = pltpu.get_barrier_semaphore()
+    for d in range(1, n):
+        pl.semaphore_signal(
+            barrier, inc=1, device_id={"ctx": lax.rem(me + d, n)}, device_id_type=MESH
+        )
+    pl.semaphore_signal(barrier, inc=1, device_id=sibling, device_id_type=MESH)
+    pl.semaphore_wait(barrier, n)
+
+    def base(chunk):
+        return pl.multiple_of(PAD + chunk * rows, 16)
+
+    def source(d):
+        return lax.rem(me + n - d, n)
+
+    def peer(d):
+        return {"ctx": lax.rem(me + d, n)}
+
+    my_half = pl.multiple_of(core * half, 16)
+    sends = []
+    for d in range(1, n):
+        copy = pltpu.make_async_remote_copy(
+            src_ref=own_ref.at[pl.ds(my_half, half)],
+            dst_ref=hid.at[pl.ds(pl.multiple_of(base(me) + my_half, 16), half)],
+            send_sem=hs_sem.at[d],
+            recv_sem=hr_sem.at[d],
+            device_id=peer(d),
+            device_id_type=MESH,
+        )
+        copy.start()
+        sends.append(copy)
+    position = lax.broadcasted_iota(jnp.int32, (rows, 4 * rows), 0)
+    byte = lax.broadcasted_iota(jnp.int32, (rows, 4 * rows), 1)
+    values = ids_ref[...].astype(F32)
+    lane = lax.broadcasted_iota(jnp.int32, (rows, 128), 1)
+    id_columns = jnp.zeros((rows, 128), F32)
+    for phase in range(4):
+        picked = jnp.where(byte == 4 * position + phase, values, 0.0)
+        column = jnp.sum(picked, axis=1, keepdims=True)
+        id_columns = jnp.where(lane == phase, column, id_columns)
+    idc[0:PAD] = jnp.zeros((PAD, 128), BF16)
+    idc[PAD + total : 2 * PAD + total] = jnp.zeros((PAD, 128), BF16)
+    idc[pl.ds(base(me), rows)] = id_columns.astype(BF16)
+    id_sends = []
+    for d in range(1, n):
+        block = idc.at[pl.ds(base(me), rows)]
+        copy = pltpu.make_async_remote_copy(
+            src_ref=block,
+            dst_ref=block,
+            send_sem=is_sem.at[d],
+            recv_sem=ir_sem.at[d],
+            device_id=peer(d),
+            device_id_type=MESH,
+        )
+        copy.start()
+        id_sends.append(copy)
+
+    for edge in (0, PAD + total):
+        hid[edge : edge + PAD] = jnp.zeros((PAD, width), BF16)
+        q_all[edge : edge + PAD] = jnp.zeros((PAD, cols), BF16)
+    hid[pl.ds(base(me), rows)] = own_ref[...]
+
+    def project(chunk):
+        x = hid[pl.ds(base(chunk), rows)]
+        at = pl.ds(pl.multiple_of(chunk * rows, 16), rows)
+        q_all[pl.ds(base(chunk), rows)] = (nn(x, wqkv[0]).astype(BF16).astype(F32) * 0.125).astype(
+            BF16
+        )
+        k_all[at] = nn(x, wqkv[1]).astype(BF16)
+        v_all[at] = nn(x, wqkv[2]).astype(BF16)
+
+    loads[0].wait()
+    project(me)
+    forwards = []
+    for d in range(1, n):
+        sends[d - 1].wait_recv()
+        block = hid.at[pl.ds(pl.multiple_of(base(source(d)) + my_half, 16), half)]
+        copy = pltpu.make_async_remote_copy(
+            src_ref=block,
+            dst_ref=block,
+            send_sem=fs_sem.at[d],
+            recv_sem=fr_sem.at[d],
+            device_id=sibling,
+            device_id_type=MESH,
+        )
+        copy.start()
+        forwards.append(copy)
+    for d in range(1, n):
+        forwards[d - 1].wait_recv()
+        project(source(d))
+
+    low = lax.broadcasted_iota(jnp.int32, (1, 128), 1) < 64
+    low16 = jnp.where(low, 1.0, 0.0).astype(BF16)
+    high16 = jnp.where(low, 0.0, 1.0).astype(BF16)
+    usable = 4 * lax.broadcasted_iota(jnp.int32, (1, total), 1) < length
+
+    def softmax_rows(q, k):
+        scores = jnp.where(usable, nt(q, k), -1e30)
+        largest = jnp.max(scores, axis=1, keepdims=True)
+        weights = jnp.exp(scores - largest)
+        totals = jnp.sum(weights, axis=1, keepdims=True)
+        return weights, largest, totals
+
+    window = pl.ds(pl.multiple_of(me * rows, 16), rows + 2 * PAD)
+
+    def trimmed(x):
+        return x.astype(F32)[PAD - HALO : PAD - HALO + win]
+
+    q_win = trimmed(q_all[window]).astype(BF16)
+    parts = []
+    for pair in range(pairs):
+        at = slice(128 * pair, 128 * pair + 128)
+        q, k, v = q_win[:, at], k_all[:, at], v_all[:, at]
+        outs = []
+        for j, mask in enumerate((low16, high16)):
+            weights, largest, totals = softmax_rows(q * mask, k)
+            inverse = 1.0 / totals
+            outs.append(nn(weights.astype(BF16), v) * inverse)
+            p_own[2 * pair + j] = (weights * inverse)[HALO : HALO + rows]
+        parts.append(jnp.where(low, outs[0], outs[1]).astype(BF16))
+    loads[1].wait()
+    tx_attn[...] = nn(jnp.concatenate(parts, axis=1), wout[...])
+
+    def swap(i, tx, rx):
+        copy = pltpu.make_async_remote_copy(
+            src_ref=tx,
+            dst_ref=rx,
+            send_sem=xs_sem.at[i],
+            recv_sem=xr_sem.at[i],
+            device_id=sibling,
+            device_id_type=MESH,
+        )
+        copy.start()
+        return copy
+
+    swap_attn = swap(0, tx_attn, rx_attn)
+    for pair in range(pairs):
+        at = slice(128 * pair, 128 * pair + 128)
+        q, k, v = q_all[PAD : PAD + total, at], k_all[:, at], v_all[:, at]
+        outs, norms = [], []
+        for mask in (low16, high16):
+            weights, largest, totals = softmax_rows(q * mask, k)
+            outs.append(nn(weights.astype(BF16), v) * (1.0 / totals))
+            norms.append(largest + jnp.log(totals))
+        attn_all[:, at] = jnp.where(low, outs[0], outs[1]).astype(BF16)
+        ln2[pair] = jnp.where(low, norms[0], norms[1])
+    loads[2].wait()
+    loads[3].wait()
+    swap_attn.wait_recv()
+    first = me * rows - HALO
+    place = first + lax.broadcasted_iota(jnp.int32, (win, 1), 0)
+    inside = jnp.logical_and(place >= 0, place < total)
+    context = trimmed(hid[window]) + (tx_attn[...] + rx_attn[...])
+    context = jnp.where(inside, context, 0.0).astype(BF16)
+    y0, y1, y2, y3 = [nn(context, wup[tap]) for tap in range(4)]
+
+    def earlier(x):
+        return pltpu.roll(x, 1, 0)
+
+    def later(x):
+        return pltpu.roll(x, win - 1, 0)
+
+    y01, y23 = y0 + y1, y2 + y3
+    pre = (earlier(y0) + y1 + y23, y01 + y23, y01 + y2 + later(y3), y01 + later(y23))
+    c0, c1 = 0.7978845608028654, 0.044715
+    for phase in range(4):
+        x = pre[phase]
+        square = x * x
+        th = jnp.tanh(c0 * (x + c1 * (x * square)))
+        gate = 0.5 * (1.0 + th)
+        active = (x * gate).astype(BF16)
+        at = slice(phase * win, phase * win + win)
+        tx_log[at] = nn(active, whead[...])
+        dgelu[at] = gate + 0.5 * x * (1.0 - th * th) * (c0 * (1.0 + 3.0 * c1 * square))
+    swap_log = swap(1, tx_log, rx_log)
+    own_keys = pl.ds(pl.multiple_of(me * rows, 16), rows)
+    key_place = me * rows + lax.broadcasted_iota(jnp.int32, (1, 128), 1) % rows
+    key_usable = 4 * key_place < length
+    for pair in range(pairs):
+        at = slice(128 * pair, 128 * pair + 128)
+        k = k_all[own_keys, at]
+        both = jnp.concatenate([k * low16, k * high16], axis=0)
+        scores = nt(q_all[PAD : PAD + total, at], both)
+        p_keys[pair] = jnp.where(key_usable, jnp.exp(scores - ln2[pair]), 0.0)
+    for copy in id_sends:
+        copy.wait_recv()
+    ids_win = trimmed(idc[window])
+    inv_length = 1.0 / jnp.full((1, 1), length, jnp.int32).astype(F32)
+    vocab = lax.broadcasted_iota(jnp.int32, (win, whead.shape[1]), 1).astype(F32)
+    swap_log.wait_recv()
+    grads = []
+    for phase in range(4):
+        at = slice(phase * win, phase * win + win)
+        logits = tx_log[at] + rx_log[at]
+        weights = jnp.exp(logits - jnp.max(logits, axis=1, keepdims=True))
+        soft = weights * (1.0 / jnp.sum(weights, axis=1, keepdims=True))
+        hot = jnp.where(vocab == ids_win[:, phase : phase + 1], 1.0, 0.0)
+        counted = jnp.logical_and(inside, 4 * place + phase < length)
+        logit_grad = ((soft - hot) * jnp.where(counted, inv_length, 0.0)).astype(BF16)
+        grad = nt(logit_grad, whead[...]) * dgelu[at]
+        grads.append(grad.astype(BF16).astype(F32))
+    g0, g1, g2, g3 = grads
+    g01, g23 = g0 + g1, g2 + g3
+    taps = (later(g0) + g1 + g23, g01 + g23, earlier(g3) + g01 + g2, earlier(g23) + g01)
+    partial = jnp.zeros((rows, width), F32)
+    for tap in range(4):
+        partial = partial + nt(taps[tap][HALO : HALO + rows].astype(BF16), wup[tap])
+    tx_ctx[...] = partial
+    swap_ctx = swap(2, tx_ctx, rx_ctx)
+    swap_ctx.wait_recv()
+    context_grad = tx_ctx[...] + rx_ctx[...]
+    ag = nt(context_grad.astype(BF16), wout[...]).astype(BF16)
+    ag_all[own_keys] = ag
+    ag_sends = []
+    for d in range(1, n):
+        block = ag_all.at[own_keys]
+        copy = pltpu.make_async_remote_copy(
+            src_ref=block,
+            dst_ref=block,
+            send_sem=as_sem.at[d],
+            recv_sem=ar_sem.at[d],
+            device_id=peer(d),
+            device_id_type=MESH,
+        )
+        copy.start()
+        ag_sends.append(copy)
+
+    def head_dots(product):
+        first_head = jnp.sum(jnp.where(low, product, 0.0), axis=1, keepdims=True)
+        second_head = jnp.sum(jnp.where(low, 0.0, product), axis=1, keepdims=True)
+        return first_head, second_head
+
+    q_grads = []
+    for pair in range(pairs):
+        at = slice(128 * pair, 128 * pair + 128)
+        g, k, v = ag[:, at], k_all[:, at], v_all[:, at]
+        dots = head_dots(g.astype(F32) * attn_all[own_keys, at].astype(F32))
+        outs = []
+        for j, mask in enumerate((low16, high16)):
+            score_grad = p_own[2 * pair + j] * (nt(g * mask, v) - dots[j])
+            outs.append(nn(score_grad.astype(BF16), k))
+        q_grads.append((jnp.where(low, outs[0], outs[1]) * 0.125).astype(BF16))
+    back = nt(jnp.concatenate(q_grads, axis=1), wqkv[0])
+    v_pairs = []
+    for pair in range(pairs):
+        v = v_all[own_keys, 128 * pair : 128 * pair + 128]
+        v_pairs.append(jnp.concatenate([v * low16, v * high16], axis=0))
+    k_sums = [jnp.zeros((128, 128), F32) for _ in range(pairs)]
+    v_sums = [jnp.zeros((128, 128), F32) for _ in range(pairs)]
+    for d in range(n):
+        if d > 0:
+            ag_sends[d - 1].wait_recv()
+        chunk = source(d) if d > 0 else me
+        block = pl.ds(pl.multiple_of(chunk * rows, 16), rows)
+        for pair in range(pairs):
+            at = slice(128 * pair, 128 * pair + 128)
+            g = ag_all[block, at]
+            dots = head_dots(g.astype(F32) * attn_all[block, at].astype(F32))
+            probs = p_keys[pair, block]
+            score_grad = probs * (nt(g, v_pairs[pair]) - jnp.where(low, dots[0], dots[1]))
+            q = q_all[pl.ds(base(chunk), rows), at]
+            k_sums[pair] = k_sums[pair] + tn(score_grad.astype(BF16), q)
+            v_sums[pair] = v_sums[pair] + tn(probs.astype(BF16), g)
+
+    def joined(sums):
+        return jnp.concatenate(
+            [jnp.where(low, s[:rows], s[rows:]).astype(BF16) for s in sums], axis=1
+        )
+
+    tx_out[...] = back + nt(joined(k_sums), wqkv[1]) + nt(joined(v_sums), wqkv[2])
+    swap_out = swap(3, tx_out, rx_out)
+    for copy in sends + forwards + id_sends + ag_sends + [swap_attn, swap_log, swap_ctx]:
+        copy.wait_send()
+    swap_out.wait()
+    out_ref[...] = (context_grad + (tx_out[...] + rx_out[...])).astype(BF16)
+
+
+def fused_body(byte_ids, lengths, hidden, w_qkv, w_out, w_up, w_head):
+    n = lax.axis_size("ctx")
+    rows, width = hidden.shape[1:]
+    total = n * rows
+    cols = w_out.shape[0]
+    vocab = w_head.shape[1]
+    win = rows + 2 * HALO
+    vmem = pl.BlockSpec(memory_space=pltpu.VMEM)
+    anywhere = pl.BlockSpec(memory_space=pl.ANY)
+    dma = pltpu.SemaphoreType.DMA
+    result = pl.pallas_call(
+        functools.partial(kernel, n),
+        out_shape=jax.ShapeDtypeStruct((rows, width), BF16),
+        in_specs=[pl.BlockSpec(memory_space=pltpu.SMEM), vmem, vmem] + [anywhere] * 4,
+        out_specs=vmem,
+        scratch_shapes=[
+            pltpu.VMEM((3, width, cols), BF16),
+            pltpu.VMEM((cols, width), BF16),
+            pltpu.VMEM((4, width, cols), BF16),
+            pltpu.VMEM((cols, vocab), BF16),
+            pltpu.VMEM((total + 2 * PAD, width), BF16),
+            pltpu.VMEM((total + 2 * PAD, 128), BF16),
+            pltpu.VMEM((total + 2 * PAD, cols), BF16),
+            pltpu.VMEM((total, cols), BF16),
+            pltpu.VMEM((total, cols), BF16),
+            pltpu.VMEM((total, cols), BF16),
+            pltpu.VMEM((cols // 128, total, 128), F32),
+            pltpu.VMEM((cols // 64, rows, total), F32),
+            pltpu.VMEM((cols // 128, total, 128), F32),
+            pltpu.VMEM((4 * win, cols), F32),
+            pltpu.VMEM((total, cols), BF16),
+            pltpu.VMEM((win, width), F32),
+            pltpu.VMEM((win, width), F32),
+            pltpu.VMEM((4 * win, vocab), F32),
+            pltpu.VMEM((4 * win, vocab), F32),
+            pltpu.VMEM((rows, width), F32),
+            pltpu.VMEM((rows, width), F32),
+            pltpu.VMEM((rows, width), F32),
+            pltpu.VMEM((rows, width), F32),
+            dma((4,)),
+        ]
+        + [dma((n,))] * 8
+        + [dma((4,))] * 2,
+        compiler_params=pltpu.CompilerParams(
+            collective_id=0, has_side_effects=True, vmem_limit_bytes=40 * 1024 * 1024
+        ),
+    )(
+        lengths,
+        byte_ids,
+        hidden[0],
+        jnp.transpose(w_qkv, (1, 0, 2)),
+        w_out,
+        w_up,
+        w_head,
+    )
+    return result[None]
+
+
+def fits(mesh, rows, cols):
+    return mesh.shape["ctx"] * rows <= 256 and rows == 64 and cols % 128 == 0 and mesh.shape["mp"] == 2
+
+
 def solution(mesh):
+    def body(*arrays):
+        rows, cols = arrays[2].shape[1], arrays[4].shape[0]
+        chosen = fused_body if fits(mesh, rows, cols) else general_body
+        return chosen(*arrays)
+
     placed = (
         P(("groups", "dp"), "ctx"),
         P(("groups", "dp")),

time: 256 us -> 39.6 us (0.15)
  blocking collectives: 93.9 us -> 0 us
  waiting for transfers between devices: 77 us -> 0 us
  Pallas kernels: 0 us -> 31.3 us
  matrix products: 28.3 us -> 0 us
  between operations: 14.2 us -> 0.67 us
  other arithmetic: 12.9 us -> 0 us
  local copies, waits for them, and re-layouts: 18.3 us -> 7.34 us
  starting transfers between devices: 10.6 us -> 0 us
    all_gather x6 -> x0, blocking collectives: 93.9 us -> none  [the longest x1 17.8 us: body(): outgrad_piece = lax.all_gather(attn_grad, 'ctx', axis=0, tiled=True)]
    psum x4 -> x0, waiting for transfers between devices: 72.7 us -> none  [pair_sum(): return lax.psum(values, 'mp')]
    pallas_call x0 -> x1, Pallas kernels: none -> 31.3 us  [fused_body(): pl.pallas_call(functools.partial(kernel, n), out_shape=jax.ShapeDtypeStru...]
    dot_general x20 -> x0, matrix products: 28.3 us -> none  [the longest x4 6.98 us: body(): jnp.dot(tap_sum, w_up[offset].T, preferred_element_type=jnp.float32)]
    ppermute x4 -> x0, starting transfers between devices: 10.5 us -> none  [the longest x2 7.88 us: with_halo(): before = lax.ppermute(last, axis, up)]
    reduce_sum x7 -> x0, other arithmetic: 6.1 us -> none  [the longest x4 3.75 us: body(): jnp.sum(window.reshape(rows, 4, split_width), axis=1).astype(jnp.bfloat16)]
    reshape x8 -> x0, local copies, waits for them, and re-layouts: 5.96 us -> none  [the longest x3 2 us: body(): window.reshape(rows, 4, split_width)]
    ppermute x4 -> x0, waiting for transfers between devices: 4.17 us -> none  [the longest x2 4.16 us: with_halo(): after = lax.ppermute(initial, axis, down)]
  transfers between devices with their start and end apart: 8 -> 0, of which waited for: 5 -> 0; matrix products, arithmetic and copies ran while one was open for 2% -> 0% of each run, Pallas kernels for 0% -> 0%
where the time goes in v1:
time: 39.6 us; the launch traced here: 39.3 us
  Pallas kernels  31.3 us (79%)
  local copies, waits for them, and re-layouts  7.34 us (19%)
  between operations  0.67 us (2%)
    pallas_call x1, Pallas kernels, fused_body(): pl.pallas_call(functools.partial(kernel, n), out_shape=jax.ShapeDtypeStru...  31.3 us
    unnamed x13, local copies, waits for them, and re-layouts  7.34 us

profile of v1, /device:TPU:0, one launch (start us, length us, event | category | flops | bytes accessed | tf_op | source)
XLA Modules:
  0.0 39.3 jit_solution(12812324566865849329)
XLA Ops:
  0.7 0.0 copy-start
  0.7 1.7 %copy-done = bf16[4,768,384]{2,1,0:T(8,128)(2,1)S(1)} copy-done((bf16[4,768,384]{2,1,0:T(8,128)(2,1)S(1)}, bf16[4,768,384]{2,1,0:T(8,128)(2,1)}, u32[]{:S(2)}) %copy-start) | copy-done | bytes 2359320
  2.3 0.0 copy-start.1
  2.3 1.5 %copy-done.1 = bf16[768,3,384]{2,0,1:T(8,128)(2,1)S(1)} copy-done((bf16[768,3,384]{2,0,1:T(8,128)(2,1)S(1)}, bf16[768,3,384]{2,0,1:T(8,128)(2,1)}, u32[]{:S(2)}) %copy-start.1) | copy-done | bytes 1769496
  3.8 0.0 copy-start.2
  3.8 1.1 %copy-done.2 = bf16[384,768]{1,0:T(8,128)(2,1)S(1)} copy-done((bf16[384,768]{1,0:T(8,128)(2,1)S(1)}, bf16[384,768]{1,0:T(8,128)(2,1)}, u32[]{:S(2)}) %copy-start.2) | copy-done | bytes 589848
  4.9 0.0 copy-start.3
  4.9 0.9 %copy-done.3 = bf16[384,256]{1,0:T(8,128)(2,1)S(1)} copy-done((bf16[384,256]{1,0:T(8,128)(2,1)S(1)}, bf16[384,256]{1,0:T(8,128)(2,1)}, u32[]{:S(2)}) %copy-start.3) | copy-done | bytes 196632
  5.8 0.0 copy-start.4
  5.8 0.9 %copy-done.4 = bf16[1,64,768]{2,1,0:T(8,128)(2,1)S(1)} copy-done((bf16[1,64,768]{2,1,0:T(8,128)(2,1)S(1)}, bf16[1,64,768]{2,1,0:T(8,128)(2,1)}, u32[]{:S(2)}) %copy-start.4) | copy-done | bytes 98328
  6.7 0.0 copy-start.5
  6.7 0.7 %copy-done.5 = s32[1,256]{1,0:T(1,128)S(1)} copy-done((s32[1,256]{1,0:T(1,128)S(1)}, s32[1,256]{1,0:T(1,128)}, u32[]{:S(2)}) %copy-start.5) | copy-done | bytes 1048
  7.4 31.3 %shard_map.73 = bf16[64,768]{1,0:T(8,128)(2,1)S(1)} custom-call(s32[1]{0:T(128)S(6)} %copy.9.len_ref, s32[1,256]{1,0:T(1,128)S(1)} %copy-done.5, bf16[64,768]{1,0:T(8,128)(2,1)S(1)} %bitcast.5, bf16[3,768,384]{2,1,0:T(8,128)(2,1)S(1)} %bitcast.3, bf16[384,768]{1,0:T(8,128)(2,1)S(1)} %copy-done.2, bf16[4,768,384]{2,1,0:T(8,128)(2,1)S(1)} %copy-done, ...), custom_call_target="tpu_custom_call" | custom-call | tf_op jit(solution)/shard_map/pallas_call | solution.py:541
  38.6 0.6 %copy.10 = bf16[1,64,768]{2,1,0:T(8,128)(2,1)} copy(bf16[1,64,768]{2,1,0:T(8,128)(2,1)S(1)} %bitcast.4) | data formatting | bytes 196608
Async XLA Ops:
  0.7 1.7 %copy-start = (bf16[4,768,384]{2,1,0:T(8,128)(2,1)S(1)}, bf16[4,768,384]{2,1,0:T(8,128)(2,1)}, u32[]{:S(2)}) copy-start(bf16[4,768,384]{2,1,0:T(8,128)(2,1)} %wup_hbm.1) | copy-start | bytes 7077892
  2.3 1.5 %copy-start.1 = (bf16[768,3,384]{2,0,1:T(8,128)(2,1)S(1)}, bf16[768,3,384]{2,0,1:T(8,128)(2,1)}, u32[]{:S(2)}) copy-start(bf16[768,3,384]{2,0,1:T(8,128)(2,1)} %param.10) | copy-start | bytes 5308420
  3.8 1.1 %copy-start.2 = (bf16[384,768]{1,0:T(8,128)(2,1)S(1)}, bf16[384,768]{1,0:T(8,128)(2,1)}, u32[]{:S(2)}) copy-start(bf16[384,768]{1,0:T(8,128)(2,1)} %wout_hbm.1) | copy-start | bytes 1769476
  4.9 0.9 %copy-start.3 = (bf16[384,256]{1,0:T(8,128)(2,1)S(1)}, bf16[384,256]{1,0:T(8,128)(2,1)}, u32[]{:S(2)}) copy-start(bf16[384,256]{1,0:T(8,128)(2,1)} %whead_hbm.1) | copy-start | bytes 589828
  5.8 0.9 %copy-start.4 = (bf16[1,64,768]{2,1,0:T(8,128)(2,1)S(1)}, bf16[1,64,768]{2,1,0:T(8,128)(2,1)}, u32[]{:S(2)}) copy-start(bf16[1,64,768]{2,1,0:T(8,128)(2,1)} %param.9) | copy-start | bytes 294916
  6.7 0.7 %copy-start.5 = (s32[1,256]{1,0:T(1,128)S(1)}, s32[1,256]{1,0:T(1,128)}, u32[]{:S(2)}) copy-start(s32[1,256]{1,0:T(1,128)} %ids_ref.1) | copy-start | bytes 3076

commit v2 on v1

--- a/solution.py
+++ b/solution.py
@@ -190,13 +190,14 @@
 def kernel(
     n,
     len_ref,
-    ids_ref,
-    own_ref,
+    ids_hbm,
+    own_hbm,
     wqkv_hbm,
     wout_hbm,
     wup_hbm,
     whead_hbm,
     out_ref,
+    ids_vmem,
     wqkv,
     wout,
     wup,
@@ -232,7 +233,7 @@
     xs_sem,
     xr_sem,
 ):
-    rows, width = own_ref.shape
+    rows, width = own_hbm.shape
     half = rows // 2
     total = n * rows
     cols = wout.shape[0]
@@ -243,10 +244,18 @@
     sibling = {"mp": 1 - core}
     length = len_ref[0]
 
+    own_rows = pl.ds(pl.multiple_of(PAD + me * rows, 16), rows)
     loads = [
         pltpu.make_async_copy(src, dst, w_sem.at[i])
         for i, (src, dst) in enumerate(
-            ((wqkv_hbm, wqkv), (wout_hbm, wout), (wup_hbm, wup), (whead_hbm, whead))
+            (
+                (ids_hbm, ids_vmem),
+                (own_hbm, hid.at[own_rows]),
+                (wqkv_hbm, wqkv),
+                (wout_hbm, wout),
+                (wup_hbm, wup),
+                (whead_hbm, whead),
+            )
         )
     ]
     for load in loads:
@@ -273,7 +282,7 @@
     sends = []
     for d in range(1, n):
         copy = pltpu.make_async_remote_copy(
-            src_ref=own_ref.at[pl.ds(my_half, half)],
+            src_ref=own_hbm.at[pl.ds(my_half, half)],
             dst_ref=hid.at[pl.ds(pl.multiple_of(base(me) + my_half, 16), half)],
             send_sem=hs_sem.at[d],
             recv_sem=hr_sem.at[d],
@@ -284,7 +293,8 @@
         sends.append(copy)
     position = lax.broadcasted_iota(jnp.int32, (rows, 4 * rows), 0)
     byte = lax.broadcasted_iota(jnp.int32, (rows, 4 * rows), 1)
-    values = ids_ref[...].astype(F32)
+    loads[0].wait()
+    values = ids_vmem[...].astype(F32)
     lane = lax.broadcasted_iota(jnp.int32, (rows, 128), 1)
     id_columns = jnp.zeros((rows, 128), F32)
     for phase in range(4):
@@ -311,7 +321,6 @@
     for edge in (0, PAD + total):
         hid[edge : edge + PAD] = jnp.zeros((PAD, width), BF16)
         q_all[edge : edge + PAD] = jnp.zeros((PAD, cols), BF16)
-    hid[pl.ds(base(me), rows)] = own_ref[...]
 
     def project(chunk):
         x = hid[pl.ds(base(chunk), rows)]
@@ -322,7 +331,8 @@
         k_all[at] = nn(x, wqkv[1]).astype(BF16)
         v_all[at] = nn(x, wqkv[2]).astype(BF16)
 
-    loads[0].wait()
+    loads[1].wait()
+    loads[2].wait()
     project(me)
     forwards = []
     for d in range(1, n):
@@ -371,22 +381,28 @@
             outs.append(nn(weights.astype(BF16), v) * inverse)
             p_own[2 * pair + j] = (weights * inverse)[HALO : HALO + rows]
         parts.append(jnp.where(low, outs[0], outs[1]).astype(BF16))
-    loads[1].wait()
-    tx_attn[...] = nn(jnp.concatenate(parts, axis=1), wout[...])
-
-    def swap(i, tx, rx):
+    loads[3].wait()
+
+    swaps = []
+
+    def swap(tx, rx, at):
         copy = pltpu.make_async_remote_copy(
-            src_ref=tx,
-            dst_ref=rx,
-            send_sem=xs_sem.at[i],
-            recv_sem=xr_sem.at[i],
+            src_ref=tx.at[at],
+            dst_ref=rx.at[at],
+            send_sem=xs_sem.at[len(swaps)],
+            recv_sem=xr_sem.at[len(swaps)],
             device_id=sibling,
             device_id_type=MESH,
         )
         copy.start()
+        swaps.append(copy)
         return copy
 
-    swap_attn = swap(0, tx_attn, rx_attn)
+    attn_win = jnp.concatenate(parts, axis=1)
+    blocks = [slice(at, at + 256) for at in range(0, width, 256)]
+    for i, at in enumerate(blocks):
+        tx_attn[i] = nn(attn_win, wout[:, at])
+        swap(tx_attn, rx_attn, i)
     for pair in range(pairs):
         at = slice(128 * pair, 128 * pair + 128)
         q, k, v = q_all[PAD : PAD + total, at], k_all[:, at], v_all[:, at]
@@ -397,13 +413,15 @@
             norms.append(largest + jnp.log(totals))
         attn_all[:, at] = jnp.where(low, outs[0], outs[1]).astype(BF16)
         ln2[pair] = jnp.where(low, norms[0], norms[1])
-    loads[2].wait()
-    loads[3].wait()
-    swap_attn.wait_recv()
+    loads[4].wait()
+    loads[5].wait()
+    for copy in swaps:
+        copy.wait_recv()
     first = me * rows - HALO
     place = first + lax.broadcasted_iota(jnp.int32, (win, 1), 0)
     inside = jnp.logical_and(place >= 0, place < total)
-    context = trimmed(hid[window]) + (tx_attn[...] + rx_attn[...])
+    added = [tx_attn[i] + rx_attn[i] for i in range(len(blocks))]
+    context = trimmed(hid[window]) + jnp.concatenate(added, axis=1)
     context = jnp.where(inside, context, 0.0).astype(BF16)
     y0, y1, y2, y3 = [nn(context, wup[tap]) for tap in range(4)]
 
@@ -416,6 +434,7 @@
     y01, y23 = y0 + y1, y2 + y3
     pre = (earlier(y0) + y1 + y23, y01 + y23, y01 + y2 + later(y3), y01 + later(y23))
     c0, c1 = 0.7978845608028654, 0.044715
+    log_swaps = []
     for phase in range(4):
         x = pre[phase]
         square = x * x
@@ -423,9 +442,9 @@
         gate = 0.5 * (1.0 + th)
         active = (x * gate).astype(BF16)
         at = slice(phase * win, phase * win + win)
-        tx_log[at] = nn(active, whead[...])
+        tx_log[phase] = nn(active, whead[...])
+        log_swaps.append(swap(tx_log, rx_log, phase))
         dgelu[at] = gate + 0.5 * x * (1.0 - th * th) * (c0 * (1.0 + 3.0 * c1 * square))
-    swap_log = swap(1, tx_log, rx_log)
     own_keys = pl.ds(pl.multiple_of(me * rows, 16), rows)
     key_place = me * rows + lax.broadcasted_iota(jnp.int32, (1, 128), 1) % rows
     key_usable = 4 * key_place < length
@@ -440,11 +459,11 @@
     ids_win = trimmed(idc[window])
     inv_length = 1.0 / jnp.full((1, 1), length, jnp.int32).astype(F32)
     vocab = lax.broadcasted_iota(jnp.int32, (win, whead.shape[1]), 1).astype(F32)
-    swap_log.wait_recv()
     grads = []
     for phase in range(4):
         at = slice(phase * win, phase * win + win)
-        logits = tx_log[at] + rx_log[at]
+        log_swaps[phase].wait_recv()
+        logits = tx_log[phase] + rx_log[phase]
         weights = jnp.exp(logits - jnp.max(logits, axis=1, keepdims=True))
         soft = weights * (1.0 / jnp.sum(weights, axis=1, keepdims=True))
         hot = jnp.where(vocab == ids_win[:, phase : phase + 1], 1.0, 0.0)
@@ -455,13 +474,16 @@
     g0, g1, g2, g3 = grads
     g01, g23 = g0 + g1, g2 + g3
     taps = (later(g0) + g1 + g23, g01 + g23, earlier(g3) + g01 + g2, earlier(g23) + g01)
-    partial = jnp.zeros((rows, width), F32)
-    for tap in range(4):
-        partial = partial + nt(taps[tap][HALO : HALO + rows].astype(BF16), wup[tap])
-    tx_ctx[...] = partial
-    swap_ctx = swap(2, tx_ctx, rx_ctx)
-    swap_ctx.wait_recv()
-    context_grad = tx_ctx[...] + rx_ctx[...]
+    taps = [x[HALO : HALO + rows].astype(BF16) for x in taps]
+    ctx_swaps = []
+    for i, at in enumerate(blocks):
+        tx_ctx[i] = (nt(taps[0], wup[0, at]) + nt(taps[1], wup[1, at])) + (
+            nt(taps[2], wup[2, at]) + nt(taps[3], wup[3, at])
+        )
+        ctx_swaps.append(swap(tx_ctx, rx_ctx, i))
+    for copy in ctx_swaps:
+        copy.wait_recv()
+    context_grad = jnp.concatenate([tx_ctx[i] + rx_ctx[i] for i in range(len(blocks))], axis=1)
     ag = nt(context_grad.astype(BF16), wout[...]).astype(BF16)
     ag_all[own_keys] = ag
     ag_sends = []
@@ -520,12 +542,16 @@
             [jnp.where(low, s[:rows], s[rows:]).astype(BF16) for s in sums], axis=1
         )
 
-    tx_out[...] = back + nt(joined(k_sums), wqkv[1]) + nt(joined(v_sums), wqkv[2])
-    swap_out = swap(3, tx_out, rx_out)
-    for copy in sends + forwards + id_sends + ag_sends + [swap_attn, swap_log, swap_ctx]:
+    k_grad, v_grad = joined(k_sums), joined(v_sums)
+    out_swaps = []
+    for i, at in enumerate(blocks):
+        tx_out[i] = back[:, at] + nt(k_grad, wqkv[1, at]) + nt(v_grad, wqkv[2, at])
+        out_swaps.append(swap(tx_out, rx_out, i))
+    for copy in sends + forwards + id_sends + ag_sends + swaps:
         copy.wait_send()
-    swap_out.wait()
-    out_ref[...] = (context_grad + (tx_out[...] + rx_out[...])).astype(BF16)
+    for i, at in enumerate(blocks):
+        out_swaps[i].wait_recv()
+        out_ref[:, at] = (context_grad[:, at] + (tx_out[i] + rx_out[i])).astype(BF16)
 
 
 def fused_body(byte_ids, lengths, hidden, w_qkv, w_out, w_up, w_head):
@@ -541,9 +567,10 @@
     result = pl.pallas_call(
         functools.partial(kernel, n),
         out_shape=jax.ShapeDtypeStruct((rows, width), BF16),
-        in_specs=[pl.BlockSpec(memory_space=pltpu.SMEM), vmem, vmem] + [anywhere] * 4,
+        in_specs=[pl.BlockSpec(memory_space=pltpu.SMEM)] + [anywhere] * 6,
         out_specs=vmem,
         scratch_shapes=[
+            pltpu.VMEM((1, 4 * rows), jnp.int32),
             pltpu.VMEM((3, width, cols), BF16),
             pltpu.VMEM((cols, width), BF16),
             pltpu.VMEM((4, width, cols), BF16),
@@ -559,20 +586,20 @@
             pltpu.VMEM((cols // 128, total, 128), F32),
             pltpu.VMEM((4 * win, cols), F32),
             pltpu.VMEM((total, cols), BF16),
-            pltpu.VMEM((win, width), F32),
-            pltpu.VMEM((win, width), F32),
-            pltpu.VMEM((4 * win, vocab), F32),
-            pltpu.VMEM((4 * win, vocab), F32),
-            pltpu.VMEM((rows, width), F32),
-            pltpu.VMEM((rows, width), F32),
-            pltpu.VMEM((rows, width), F32),
-            pltpu.VMEM((rows, width), F32),
-            dma((4,)),
+            pltpu.VMEM((width // 256, win, 256), F32),
+            pltpu.VMEM((width // 256, win, 256), F32),
+            pltpu.VMEM((4, win, vocab), F32),
+            pltpu.VMEM((4, win, vocab), F32),
+            pltpu.VMEM((width // 256, rows, 256), F32),
+            pltpu.VMEM((width // 256, rows, 256), F32),
+            pltpu.VMEM((width // 256, rows, 256), F32),
+            pltpu.VMEM((width // 256, rows, 256), F32),
+            dma((6,)),
         ]
         + [dma((n,))] * 8
-        + [dma((4,))] * 2,
+        + [dma((3 * (width // 256) + 4,))] * 2,
         compiler_params=pltpu.CompilerParams(
-            collective_id=0, has_side_effects=True, vmem_limit_bytes=40 * 1024 * 1024
+            collective_id=0, has_side_effects=True, vmem_limit_bytes=60 * 1024 * 1024
         ),
     )(
         lengths,
@@ -586,14 +613,14 @@
     return result[None]
 
 
-def fits(mesh, rows, cols):
-    return mesh.shape["ctx"] * rows <= 256 and rows == 64 and cols % 128 == 0 and mesh.shape["mp"] == 2
+def fits(mesh, rows, width, cols):
+    return mesh.shape["ctx"] * rows <= 256 and rows == 64 and cols % 128 == 0 and width % 256 == 0 and mesh.shape["mp"] == 2
 
 
 def solution(mesh):
     def body(*arrays):
-        rows, cols = arrays[2].shape[1], arrays[4].shape[0]
-        chosen = fused_body if fits(mesh, rows, cols) else general_body
+        (_, rows, width), cols = arrays[2].shape, arrays[4].shape[0]
+        chosen = fused_body if fits(mesh, rows, width, cols) else general_body
         return chosen(*arrays)
 
     placed = (

time: 39.6 us -> 34.5 us (0.87)
  local copies, waits for them, and re-layouts: 7.34 us -> 1.54 us
  Pallas kernels: 31.3 us -> 32.2 us
    unnamed x13 -> x1, local copies, waits for them, and re-layouts: 7.34 us -> 1.54 us
    pallas_call x1, Pallas kernels: 31.3 us -> 32.2 us  [fused_body(): pl.pallas_call(functools.partial(kernel, n), out_shape=jax.ShapeDtypeStru...]
where the time goes in v2:
time: 34.5 us; the launch traced here: 34.4 us
  Pallas kernels  32.2 us (93%)
  local copies, waits for them, and re-layouts  1.54 us (4%)
  between operations  0.66 us (2%)
    pallas_call x1, Pallas kernels, fused_body(): pl.pallas_call(functools.partial(kernel, n), out_shape=jax.ShapeDtypeStru...  32.2 us
    unnamed x1, local copies, waits for them, and re-layouts  1.54 us

profile of v2, /device:TPU:0, one launch (start us, length us, event | category | flops | bytes accessed | tf_op | source)
XLA Modules:
  0.0 34.4 jit_solution(15803943269953679578)
XLA Ops:
  0.7 32.2 %shard_map.73 = bf16[64,768]{1,0:T(8,128)(2,1)} custom-call(s32[1]{0:T(128)S(6)} %copy.9.len_ref, s32[1,256]{1,0:T(1,128)} %ids_hbm.1, bf16[64,768]{1,0:T(8,128)(2,1)} %bitcast.5, bf16[3,768,384]{2,1,0:T(8,128)(2,1)} %bitcast.3, bf16[384,768]{1,0:T(8,128)(2,1)} %wout_hbm.1, bf16[4,768,384]{2,1,0:T(8,128)(2,1)} %wup_hbm.1, bf16[384,256]{1,0:T(8,128)(2,1)} %whead_hbm.1), custom_call_target="tpu_custom_call" | custom-call | tf_op jit(solution)/shard_map/pallas_call | solution.py:567
  32.8 1.5 %copy.10 = bf16[1,64,768]{2,1,0:T(8,128)(2,1)} copy(bf16[1,64,768]{2,1,0:T(8,128)(2,1)} %bitcast.4) | data formatting | bytes 196608

commit v3 on v2

--- a/solution.py
+++ b/solution.py
@@ -197,13 +197,12 @@
     wup_hbm,
     whead_hbm,
     out_ref,
-    ids_vmem,
+    ids,
     wqkv,
     wout,
     wup,
     whead,
     hid,
-    idc,
     q_all,
     k_all,
     v_all,
@@ -249,7 +248,7 @@
         pltpu.make_async_copy(src, dst, w_sem.at[i])
         for i, (src, dst) in enumerate(
             (
-                (ids_hbm, ids_vmem),
+                (ids_hbm, ids.at[1]),
                 (own_hbm, hid.at[own_rows]),
                 (wqkv_hbm, wqkv),
                 (wout_hbm, wout),
@@ -291,25 +290,11 @@
         )
         copy.start()
         sends.append(copy)
-    position = lax.broadcasted_iota(jnp.int32, (rows, 4 * rows), 0)
-    byte = lax.broadcasted_iota(jnp.int32, (rows, 4 * rows), 1)
-    loads[0].wait()
-    values = ids_vmem[...].astype(F32)
-    lane = lax.broadcasted_iota(jnp.int32, (rows, 128), 1)
-    id_columns = jnp.zeros((rows, 128), F32)
-    for phase in range(4):
-        picked = jnp.where(byte == 4 * position + phase, values, 0.0)
-        column = jnp.sum(picked, axis=1, keepdims=True)
-        id_columns = jnp.where(lane == phase, column, id_columns)
-    idc[0:PAD] = jnp.zeros((PAD, 128), BF16)
-    idc[PAD + total : 2 * PAD + total] = jnp.zeros((PAD, 128), BF16)
-    idc[pl.ds(base(me), rows)] = id_columns.astype(BF16)
     id_sends = []
-    for d in range(1, n):
-        block = idc.at[pl.ds(base(me), rows)]
+    for d, slot in ((1, 0), (n - 1, 2)):
         copy = pltpu.make_async_remote_copy(
-            src_ref=block,
-            dst_ref=block,
+            src_ref=ids_hbm,
+            dst_ref=ids.at[slot],
             send_sem=is_sem.at[d],
             recv_sem=ir_sem.at[d],
             device_id=peer(d),
@@ -331,8 +316,8 @@
         k_all[at] = nn(x, wqkv[1]).astype(BF16)
         v_all[at] = nn(x, wqkv[2]).astype(BF16)
 
-    loads[1].wait()
-    loads[2].wait()
+    for load in loads[:3]:
+        load.wait()
     project(me)
     forwards = []
     for d in range(1, n):
@@ -456,7 +441,14 @@
         p_keys[pair] = jnp.where(key_usable, jnp.exp(scores - ln2[pair]), 0.0)
     for copy in id_sends:
         copy.wait_recv()
-    ids_win = trimmed(idc[window])
+    byte = 4 * (lax.broadcasted_iota(jnp.int32, (win, 4 * rows), 0) - HALO)
+    offset = byte - lax.broadcasted_iota(jnp.int32, (win, 4 * rows), 1)
+    ids_win = []
+    for phase in range(4):
+        found = jnp.zeros((win, 4 * rows), jnp.int32)
+        for side in range(3):
+            found = found + jnp.where(offset == 4 * rows * (side - 1) - phase, ids[side], 0)
+        ids_win.append(jnp.sum(found.astype(F32), axis=1, keepdims=True))
     inv_length = 1.0 / jnp.full((1, 1), length, jnp.int32).astype(F32)
     vocab = lax.broadcasted_iota(jnp.int32, (win, whead.shape[1]), 1).astype(F32)
     grads = []
@@ -466,7 +458,7 @@
         logits = tx_log[phase] + rx_log[phase]
         weights = jnp.exp(logits - jnp.max(logits, axis=1, keepdims=True))
         soft = weights * (1.0 / jnp.sum(weights, axis=1, keepdims=True))
-        hot = jnp.where(vocab == ids_win[:, phase : phase + 1], 1.0, 0.0)
+        hot = jnp.where(vocab == ids_win[phase], 1.0, 0.0)
         counted = jnp.logical_and(inside, 4 * place + phase < length)
         logit_grad = ((soft - hot) * jnp.where(counted, inv_length, 0.0)).astype(BF16)
         grad = nt(logit_grad, whead[...]) * dgelu[at]
@@ -570,13 +562,12 @@
         in_specs=[pl.BlockSpec(memory_space=pltpu.SMEM)] + [anywhere] * 6,
         out_specs=vmem,
         scratch_shapes=[
-            pltpu.VMEM((1, 4 * rows), jnp.int32),
+            pltpu.VMEM((3, 1, 4 * rows), jnp.int32),
             pltpu.VMEM((3, width, cols), BF16),
             pltpu.VMEM((cols, width), BF16),
             pltpu.VMEM((4, width, cols), BF16),
             pltpu.VMEM((cols, vocab), BF16),
             pltpu.VMEM((total + 2 * PAD, width), BF16),
-            pltpu.VMEM((total + 2 * PAD, 128), BF16),
             pltpu.VMEM((total + 2 * PAD, cols), BF16),
             pltpu.VMEM((total, cols), BF16),
             pltpu.VMEM((total, cols), BF16),
@@ -614,7 +605,7 @@
 
 
 def fits(mesh, rows, width, cols):
-    return mesh.shape["ctx"] * rows <= 256 and rows == 64 and cols % 128 == 0 and width % 256 == 0 and mesh.shape["mp"] == 2
+    return 3 <= mesh.shape["ctx"] <= 4 and rows == 64 and cols % 128 == 0 and width % 256 == 0 and mesh.shape["mp"] == 2
 
 
 def solution(mesh):

time: 34.5 us -> 33.6 us (0.974)
  Pallas kernels: 32.2 us -> 31.2 us
    pallas_call x1, Pallas kernels: 32.2 us -> 31.2 us  [fused_body(): pl.pallas_call(functools.partial(kernel, n), out_shape=jax.ShapeDtypeStru...]
where the time goes in v3:
time: 33.6 us; the launch traced here: 33.4 us
  Pallas kernels  31.2 us (93%)
  local copies, waits for them, and re-layouts  1.54 us (5%)
  between operations  0.66 us (2%)
    pallas_call x1, Pallas kernels, fused_body(): pl.pallas_call(functools.partial(kernel, n), out_shape=jax.ShapeDtypeStru...  31.2 us
    unnamed x1, local copies, waits for them, and re-layouts  1.54 us

profile of v3, /device:TPU:0, one launch (start us, length us, event | category | flops | bytes accessed | tf_op | source)
XLA Modules:
  0.0 33.4 jit_solution(17919957183670830549)
XLA Ops:
  0.7 31.2 %shard_map.73 = bf16[64,768]{1,0:T(8,128)(2,1)} custom-call(s32[1]{0:T(128)S(6)} %copy.9.len_ref, s32[1,256]{1,0:T(1,128)} %ids_hbm.1, bf16[64,768]{1,0:T(8,128)(2,1)} %bitcast.5, bf16[3,768,384]{2,1,0:T(8,128)(2,1)} %bitcast.3, bf16[384,768]{1,0:T(8,128)(2,1)} %wout_hbm.1, bf16[4,768,384]{2,1,0:T(8,128)(2,1)} %wup_hbm.1, bf16[384,256]{1,0:T(8,128)(2,1)} %whead_hbm.1), custom_call_target="tpu_custom_call" | custom-call | tf_op jit(solution)/shard_map/pallas_call | solution.py:559
  31.9 1.5 %copy.10 = bf16[1,64,768]{2,1,0:T(8,128)(2,1)} copy(bf16[1,64,768]{2,1,0:T(8,128)(2,1)} %bitcast.4) | data formatting | bytes 196608

commit v4 on v3

--- a/solution.py
+++ b/solution.py
@@ -388,7 +388,7 @@
     for i, at in enumerate(blocks):
         tx_attn[i] = nn(attn_win, wout[:, at])
         swap(tx_attn, rx_attn, i)
-    for pair in range(pairs):
+    def document_forward(pair):
         at = slice(128 * pair, 128 * pair + 128)
         q, k, v = q_all[PAD : PAD + total, at], k_all[:, at], v_all[:, at]
         outs, norms = [], []
@@ -398,6 +398,9 @@
             norms.append(largest + jnp.log(totals))
         attn_all[:, at] = jnp.where(low, outs[0], outs[1]).astype(BF16)
         ln2[pair] = jnp.where(low, norms[0], norms[1])
+
+    for pair in range(pairs - 1):
+        document_forward(pair)
     loads[4].wait()
     loads[5].wait()
     for copy in swaps:
@@ -433,12 +436,15 @@
     own_keys = pl.ds(pl.multiple_of(me * rows, 16), rows)
     key_place = me * rows + lax.broadcasted_iota(jnp.int32, (1, 128), 1) % rows
     key_usable = 4 * key_place < length
-    for pair in range(pairs):
+    def key_probs(pair):
         at = slice(128 * pair, 128 * pair + 128)
         k = k_all[own_keys, at]
         both = jnp.concatenate([k * low16, k * high16], axis=0)
         scores = nt(q_all[PAD : PAD + total, at], both)
         p_keys[pair] = jnp.where(key_usable, jnp.exp(scores - ln2[pair]), 0.0)
+
+    for pair in range(pairs - 1):
+        key_probs(pair)
     for copy in id_sends:
         copy.wait_recv()
     byte = 4 * (lax.broadcasted_iota(jnp.int32, (win, 4 * rows), 0) - HALO)
@@ -473,6 +479,8 @@
             nt(taps[2], wup[2, at]) + nt(taps[3], wup[3, at])
         )
         ctx_swaps.append(swap(tx_ctx, rx_ctx, i))
+    document_forward(pairs - 1)
+    key_probs(pairs - 1)
     for copy in ctx_swaps:
         copy.wait_recv()
     context_grad = jnp.concatenate([tx_ctx[i] + rx_ctx[i] for i in range(len(blocks))], axis=1)

time: 33.6 us -> 33.5 us (level)
  no operation moved by 1% of the time
where the time goes in v4:
time: 33.5 us; the launch traced here: 33.3 us
  Pallas kernels  31.1 us (93%)
  local copies, waits for them, and re-layouts  1.54 us (5%)
  between operations  0.66 us (2%)
    pallas_call x1, Pallas kernels, fused_body(): pl.pallas_call(functools.partial(kernel, n), out_shape=jax.ShapeDtypeStru...  31.1 us
    unnamed x1, local copies, waits for them, and re-layouts  1.54 us

profile of v4, /device:TPU:0, one launch (start us, length us, event | category | flops | bytes accessed | tf_op | source)
XLA Modules:
  0.0 33.3 jit_solution(15861601176967082655)
XLA Ops:
  0.7 31.1 %shard_map.73 = bf16[64,768]{1,0:T(8,128)(2,1)} custom-call(s32[1]{0:T(128)S(6)} %copy.9.len_ref, s32[1,256]{1,0:T(1,128)} %ids_hbm.1, bf16[64,768]{1,0:T(8,128)(2,1)} %bitcast.5, bf16[3,768,384]{2,1,0:T(8,128)(2,1)} %bitcast.3, bf16[384,768]{1,0:T(8,128)(2,1)} %wout_hbm.1, bf16[4,768,384]{2,1,0:T(8,128)(2,1)} %wup_hbm.1, bf16[384,256]{1,0:T(8,128)(2,1)} %whead_hbm.1), custom_call_target="tpu_custom_call" | custom-call | tf_op jit(solution)/shard_map/pallas_call | solution.py:567
  31.8 1.5 %copy.10 = bf16[1,64,768]{2,1,0:T(8,128)(2,1)} copy(bf16[1,64,768]{2,1,0:T(8,128)(2,1)} %bitcast.4) | data formatting | bytes 196608
